TPU v7x, 256 devices: a whole 4x4x8 slice. The times are simulated.
256 devices in a mesh: rep: 8 (over z_hi, core), mod: 32 (over x, y, z_lo).
Axes of the slice: x: 4, y: 4, z: 8 (z_hi: 4, z_lo: 2; z = z_hi * 2 + z_lo), core: 2. Of those that a mesh axis runs over, the one named last changes fastest.
Arguments:
- table: float32 [64, 2048, 128], P('mod', 'rep'), may hold values from -3 to 3
- accum: float32 [64, 2048], P('mod', 'rep'), may hold values from 0.1 to 10
- bag_rows: int32 [32768, 64, 16], P(('rep', 'mod')), may hold values from 0 to 2047
- pooled_grad: bfloat16 [32768, 64, 128], P(('rep', 'mod')), may hold values from -0.59765625 to 0.59765625
Outputs:
- pooled: bfloat16 [32768, 64, 128], P(('rep', 'mod'))
- new_table: float32 [64, 2048, 128], P('mod')
- new_accum: float32 [64, 2048], P('mod')
All inputs are finite; a program needn't handle non-finite values.
Results may differ from a plain program's by a relative error of at most 0.0055.
Values may be sent and summed in bfloat16 or wider, within the bound.
A program may use at most 64 MiB of HBM per device.

v0:
```python
import math

import jax
import jax.numpy as jnp
from jax import lax
from jax.sharding import PartitionSpec as P


def shortened(value):
    return jax.tree.map(lambda a: a.astype(jnp.bfloat16) if a.dtype == jnp.float32 else a, value)


def pool_and_grad(lookup, group_rows, group_grad):
    owned, total_rows, width = lookup.shape
    group_size = group_rows.shape[0]
    pool_len = group_rows.shape[2]
    block = math.gcd(group_size, 512)
    blocks = group_size // block
    ids_blocks = group_rows.reshape(blocks, block, owned, pool_len)
    cot_blocks = group_grad.reshape(blocks, block, owned, width)
    row_iota = lax.broadcasted_iota(jnp.int32, (1, total_rows), 1)

    def step(carry, inputs):
        ids_blk, cot_blk = inputs
        outputs = []
        sums = []
        for owned_index in range(owned):
            ids_one = ids_blk[:, owned_index, :]
            counts = jnp.zeros((block, total_rows), jnp.float32)
            for slot in range(pool_len):
                counts = counts + (ids_one[:, slot : slot + 1] == row_iota).astype(jnp.float32)
            counts_low = counts.astype(jnp.bfloat16)
            pooled_one = jnp.dot(
                counts_low, lookup[owned_index], preferred_element_type=jnp.float32
            )
            outputs.append(pooled_one.astype(jnp.bfloat16))
            grad_one = lax.dot_general(
                counts_low,
                cot_blk[:, owned_index, :],
                (((0,), (0,)), ((), ())),
                preferred_element_type=jnp.float32,
            )
            sums.append(carry[owned_index] + grad_one)
        return (jnp.stack(sums), jnp.stack(outputs, axis=1))

    start = jnp.zeros((owned, total_rows, width), jnp.float32)
    row_grad, pooled_blocks = lax.scan(step, start, (ids_blocks, cot_blocks))
    return (pooled_blocks.reshape(group_size, owned, width), row_grad)


def adagrad(weights, sums, grad):
    new_sums = sums + jnp.mean(grad * grad, axis=-1)
    new_weights = weights - 0.1 * grad / jnp.sqrt(new_sums)[:, :, None]
    return (new_weights, new_sums)


def local(table, accum, bag_rows, pooled_grad):
    full_table, full_accum = (
        lax.all_gather(table, "rep", axis=1, tiled=True),
        lax.all_gather(accum, "rep", axis=1, tiled=True),
    )
    lookup = full_table.astype(jnp.bfloat16)
    group_rows = lax.all_to_all(bag_rows, "mod", split_axis=1, concat_axis=0, tiled=True)
    group_grad = lax.all_to_all(pooled_grad, "mod", split_axis=1, concat_axis=0, tiled=True)
    pooled_local, row_grad = pool_and_grad(lookup, group_rows, group_grad)
    pooled = lax.all_to_all(
        shortened(pooled_local), "mod", split_axis=0, concat_axis=1, tiled=True
    ).astype(pooled_local.dtype)
    total = lax.psum(row_grad.astype(jnp.bfloat16), "rep").astype(jnp.float32)
    new_table, new_accum = adagrad(full_table, full_accum, total)
    return (pooled, new_table, new_accum)


def solution(mesh):
    in_specs = (
        P("mod", "rep", None),
        P("mod", "rep"),
        P(("rep", "mod"), None, None),
        P(("rep", "mod"), None, None),
    )
    out_specs = (P(("rep", "mod"), None, None), P("mod", None, None), P("mod", None))
    return jax.shard_map(local, mesh=mesh, in_specs=in_specs, out_specs=out_specs, check_vma=False)
```

profile of v0, /device:TPU:1, one launch (start us, length us, event | category | flops | bytes accessed | tf_op | source)
XLA Modules:
  0.0 510.1 jit_solution(5372637380380150456)
XLA Ops:
  7.2 9.2 %all-to-all-start = ((s32[128,64,16]{0,2,1:T(8,128)}), s32[128,64,16]{0,2,1:T(8,128)S(1)}, u32[]{:S(2)}, u32[]{:S(2)}) async-start(s32[128,64,16]{0,2,1:T(8,128)} %param.8), calls=%async_computation | async-start | bytes 1048576 | tf_op jit(solution)/shard_map/all_to_all | solution.py:63
  32.6 46.6 %all-gather.2.cloned.1.call-done = f32[2,2048,128]{2,1,0:T(8,128)} async-done(((f32[2,256,128]{2,1,0:T(8,128)}), f32[2,2048,128]{2,1,0:T(8,128)}) %all-gather.2.cloned.1.call-update) | async-done | bytes 2097168 | tf_op jit(solution)/shard_map/all_gather | solution.py:59
  83.6 314.6 %while.14 = (s32[]{:T(128)}, f32[2,2048,128]{2,1,0:T(8,128)S(1)}, bf16[8,512,2,128]{3,1,0,2:T(8,128)(2,1)}, s32[8,512,2,16]{1,0,3,2:T(8,128)S(1)}, bf16[8,512,2,...) while((s32[]{:T(128)}, f32[2,2048,128]{2,1,0:T(8,128)S(1)}, ...), condition=%wide.region_1.2_spmd.clone.clone, body=%wide.region_0.1_spmd.clone.clone.sunk | while | flops 1276772352 | bytes 15860337 | solution.py:47
  84.0 9.7 %fusion.32 = bf16[512,1,128]{2,0,1:T(8,128)(2,1)S(1)} fusion(bf16[2,2048,128]{2,1,0:T(8,128)(2,1)} %get-tuple-element.403, s32[512]{0:T(512)S(1)} %bitcast.192, s32[512]{0:T(512)S(1)} %bitcast.194, s32[512]{0:T(512)S(1)} %bitcast.196, s32[512]{0:T(512)S(1)} %bitcast.198, s32[512]{0:T(512)S(1)} %bitcast.200, s32[512]{0:T(512)S(1)} %bitcast.202, ...), kind=kOutput, calls=%fused_computation.43.clone.1 | convolution fusion | flops 318832640 | bytes 688128 | tf_op jit(solution)/shard_map/while/body/eval_jaxpr/dot_general | solution.py:33
  93.8 9.2 %fusion.33 = bf16[512,1,128]{2,0,1:T(8,128)(2,1)S(1)} fusion(bf16[2,2048,128]{2,1,0:T(8,128)(2,1)S(1)} %copy-done.1, s32[512]{0:T(512)S(1)} %bitcast.224, s32[512]{0:T(512)S(1)} %bitcast.226, s32[512]{0:T(512)S(1)} %bitcast.228, s32[512]{0:T(512)S(1)} %bitcast.230, s32[512]{0:T(512)S(1)} %bitcast.232, s32[512]{0:T(512)S(1)} %bitcast.234, ...), kind=kOutput, calls=%fused_computation.42.clone.1 | convolution fusion | flops 318832640 | bytes 688128 | tf_op jit(solution)/shard_map/while/body/eval_jaxpr/dot_general | solution.py:33
  123.1 9.7 %fusion.32 = bf16[512,1,128]{2,0,1:T(8,128)(2,1)S(1)} fusion(bf16[2,2048,128]{2,1,0:T(8,128)(2,1)} %get-tuple-element.403, s32[512]{0:T(512)S(1)} %bitcast.192, s32[512]{0:T(512)S(1)} %bitcast.194, s32[512]{0:T(512)S(1)} %bitcast.196, s32[512]{0:T(512)S(1)} %bitcast.198, s32[512]{0:T(512)S(1)} %bitcast.200, s32[512]{0:T(512)S(1)} %bitcast.202, ...), kind=kOutput, calls=%fused_computation.43.clone.1 | convolution fusion | flops 318832640 | bytes 688128 | tf_op jit(solution)/shard_map/while/body/eval_jaxpr/dot_general | solution.py:33
  143.4 9.2 %fusion.31 = f32[1,2048,128]{2,1,0:T(8,128)S(1)} fusion(f32[2,2048,128]{2,1,0:T(8,128)S(1)} %get-tuple-element.392, bf16[512,2,128]{2,0,1:T(8,128)(2,1)S(1)} %dynamic-slice_bitcast_fusion.2, s32[512]{0:T(512)S(1)} %bitcast.225, s32[512]{0:T(512)S(1)} %bitcast.227, s32[512]{0:T(512)S(1)} %bitcast.229, s32[512]{0:T(512)S(1)} %bitcast.231, ...), kind=kOutput, calls=%fused_computation.38.clone.1 | convolution fusion | flops 319029248 | bytes 2260992 | tf_op jit(solution)/shard_map/while/body/eval_jaxpr/dot_general | solution.py:37
  161.8 9.7 %fusion.32 = bf16[512,1,128]{2,0,1:T(8,128)(2,1)S(1)} fusion(bf16[2,2048,128]{2,1,0:T(8,128)(2,1)} %get-tuple-element.403, s32[512]{0:T(512)S(1)} %bitcast.192, s32[512]{0:T(512)S(1)} %bitcast.194, s32[512]{0:T(512)S(1)} %bitcast.196, s32[512]{0:T(512)S(1)} %bitcast.198, s32[512]{0:T(512)S(1)} %bitcast.200, s32[512]{0:T(512)S(1)} %bitcast.202, ...), kind=kOutput, calls=%fused_computation.43.clone.1 | convolution fusion | flops 318832640 | bytes 688128 | tf_op jit(solution)/shard_map/while/body/eval_jaxpr/dot_general | solution.py:33
  171.5 9.0 %fusion.33 = bf16[512,1,128]{2,0,1:T(8,128)(2,1)S(1)} fusion(bf16[2,2048,128]{2,1,0:T(8,128)(2,1)S(1)} %copy-done.1, s32[512]{0:T(512)S(1)} %bitcast.224, s32[512]{0:T(512)S(1)} %bitcast.226, s32[512]{0:T(512)S(1)} %bitcast.228, s32[512]{0:T(512)S(1)} %bitcast.230, s32[512]{0:T(512)S(1)} %bitcast.232, s32[512]{0:T(512)S(1)} %bitcast.234, ...), kind=kOutput, calls=%fused_computation.42.clone.1 | convolution fusion | flops 318832640 | bytes 688128 | tf_op jit(solution)/shard_map/while/body/eval_jaxpr/dot_general | solution.py:33
  182.3 8.9 %fusion.31 = f32[1,2048,128]{2,1,0:T(8,128)S(1)} fusion(f32[2,2048,128]{2,1,0:T(8,128)S(1)} %get-tuple-element.392, bf16[512,2,128]{2,0,1:T(8,128)(2,1)S(1)} %dynamic-slice_bitcast_fusion.2, s32[512]{0:T(512)S(1)} %bitcast.225, s32[512]{0:T(512)S(1)} %bitcast.227, s32[512]{0:T(512)S(1)} %bitcast.229, s32[512]{0:T(512)S(1)} %bitcast.231, ...), kind=kOutput, calls=%fused_computation.38.clone.1 | convolution fusion | flops 319029248 | bytes 2260992 | tf_op jit(solution)/shard_map/while/body/eval_jaxpr/dot_general | solution.py:37
  200.7 9.7 %fusion.32 = bf16[512,1,128]{2,0,1:T(8,128)(2,1)S(1)} fusion(bf16[2,2048,128]{2,1,0:T(8,128)(2,1)} %get-tuple-element.403, s32[512]{0:T(512)S(1)} %bitcast.192, s32[512]{0:T(512)S(1)} %bitcast.194, s32[512]{0:T(512)S(1)} %bitcast.196, s32[512]{0:T(512)S(1)} %bitcast.198, s32[512]{0:T(512)S(1)} %bitcast.200, s32[512]{0:T(512)S(1)} %bitcast.202, ...), kind=kOutput, calls=%fused_computation.43.clone.1 | convolution fusion | flops 318832640 | bytes 688128 | tf_op jit(solution)/shard_map/while/body/eval_jaxpr/dot_general | solution.py:33
  220.9 9.2 %fusion.31 = f32[1,2048,128]{2,1,0:T(8,128)S(1)} fusion(f32[2,2048,128]{2,1,0:T(8,128)S(1)} %get-tuple-element.392, bf16[512,2,128]{2,0,1:T(8,128)(2,1)S(1)} %dynamic-slice_bitcast_fusion.2, s32[512]{0:T(512)S(1)} %bitcast.225, s32[512]{0:T(512)S(1)} %bitcast.227, s32[512]{0:T(512)S(1)} %bitcast.229, s32[512]{0:T(512)S(1)} %bitcast.231, ...), kind=kOutput, calls=%fused_computation.38.clone.1 | convolution fusion | flops 319029248 | bytes 2260992 | tf_op jit(solution)/shard_map/while/body/eval_jaxpr/dot_general | solution.py:37
  239.3 9.7 %fusion.32 = bf16[512,1,128]{2,0,1:T(8,128)(2,1)S(1)} fusion(bf16[2,2048,128]{2,1,0:T(8,128)(2,1)} %get-tuple-element.403, s32[512]{0:T(512)S(1)} %bitcast.192, s32[512]{0:T(512)S(1)} %bitcast.194, s32[512]{0:T(512)S(1)} %bitcast.196, s32[512]{0:T(512)S(1)} %bitcast.198, s32[512]{0:T(512)S(1)} %bitcast.200, s32[512]{0:T(512)S(1)} %bitcast.202, ...), kind=kOutput, calls=%fused_computation.43.clone.1 | convolution fusion | flops 318832640 | bytes 688128 | tf_op jit(solution)/shard_map/while/body/eval_jaxpr/dot_general | solution.py:33
  249.1 9.0 %fusion.33 = bf16[512,1,128]{2,0,1:T(8,128)(2,1)S(1)} fusion(bf16[2,2048,128]{2,1,0:T(8,128)(2,1)S(1)} %copy-done.1, s32[512]{0:T(512)S(1)} %bitcast.224, s32[512]{0:T(512)S(1)} %bitcast.226, s32[512]{0:T(512)S(1)} %bitcast.228, s32[512]{0:T(512)S(1)} %bitcast.230, s32[512]{0:T(512)S(1)} %bitcast.232, s32[512]{0:T(512)S(1)} %bitcast.234, ...), kind=kOutput, calls=%fused_computation.42.clone.1 | convolution fusion | flops 318832640 | bytes 688128 | tf_op jit(solution)/shard_map/while/body/eval_jaxpr/dot_general | solution.py:33
  259.8 8.9 %fusion.31 = f32[1,2048,128]{2,1,0:T(8,128)S(1)} fusion(f32[2,2048,128]{2,1,0:T(8,128)S(1)} %get-tuple-element.392, bf16[512,2,128]{2,0,1:T(8,128)(2,1)S(1)} %dynamic-slice_bitcast_fusion.2, s32[512]{0:T(512)S(1)} %bitcast.225, s32[512]{0:T(512)S(1)} %bitcast.227, s32[512]{0:T(512)S(1)} %bitcast.229, s32[512]{0:T(512)S(1)} %bitcast.231, ...), kind=kOutput, calls=%fused_computation.38.clone.1 | convolution fusion | flops 319029248 | bytes 2260992 | tf_op jit(solution)/shard_map/while/body/eval_jaxpr/dot_general | solution.py:37
  278.2 9.7 %fusion.32 = bf16[512,1,128]{2,0,1:T(8,128)(2,1)S(1)} fusion(bf16[2,2048,128]{2,1,0:T(8,128)(2,1)} %get-tuple-element.403, s32[512]{0:T(512)S(1)} %bitcast.192, s32[512]{0:T(512)S(1)} %bitcast.194, s32[512]{0:T(512)S(1)} %bitcast.196, s32[512]{0:T(512)S(1)} %bitcast.198, s32[512]{0:T(512)S(1)} %bitcast.200, s32[512]{0:T(512)S(1)} %bitcast.202, ...), kind=kOutput, calls=%fused_computation.43.clone.1 | convolution fusion | flops 318832640 | bytes 688128 | tf_op jit(solution)/shard_map/while/body/eval_jaxpr/dot_general | solution.py:33
  298.5 9.2 %fusion.31 = f32[1,2048,128]{2,1,0:T(8,128)S(1)} fusion(f32[2,2048,128]{2,1,0:T(8,128)S(1)} %get-tuple-element.392, bf16[512,2,128]{2,0,1:T(8,128)(2,1)S(1)} %dynamic-slice_bitcast_fusion.2, s32[512]{0:T(512)S(1)} %bitcast.225, s32[512]{0:T(512)S(1)} %bitcast.227, s32[512]{0:T(512)S(1)} %bitcast.229, s32[512]{0:T(512)S(1)} %bitcast.231, ...), kind=kOutput, calls=%fused_computation.38.clone.1 | convolution fusion | flops 319029248 | bytes 2260992 | tf_op jit(solution)/shard_map/while/body/eval_jaxpr/dot_general | solution.py:37
  316.9 9.7 %fusion.32 = bf16[512,1,128]{2,0,1:T(8,128)(2,1)S(1)} fusion(bf16[2,2048,128]{2,1,0:T(8,128)(2,1)} %get-tuple-element.403, s32[512]{0:T(512)S(1)} %bitcast.192, s32[512]{0:T(512)S(1)} %bitcast.194, s32[512]{0:T(512)S(1)} %bitcast.196, s32[512]{0:T(512)S(1)} %bitcast.198, s32[512]{0:T(512)S(1)} %bitcast.200, s32[512]{0:T(512)S(1)} %bitcast.202, ...), kind=kOutput, calls=%fused_computation.43.clone.1 | convolution fusion | flops 318832640 | bytes 688128 | tf_op jit(solution)/shard_map/while/body/eval_jaxpr/dot_general | solution.py:33
  326.7 9.0 %fusion.33 = bf16[512,1,128]{2,0,1:T(8,128)(2,1)S(1)} fusion(bf16[2,2048,128]{2,1,0:T(8,128)(2,1)S(1)} %copy-done.1, s32[512]{0:T(512)S(1)} %bitcast.224, s32[512]{0:T(512)S(1)} %bitcast.226, s32[512]{0:T(512)S(1)} %bitcast.228, s32[512]{0:T(512)S(1)} %bitcast.230, s32[512]{0:T(512)S(1)} %bitcast.232, s32[512]{0:T(512)S(1)} %bitcast.234, ...), kind=kOutput, calls=%fused_computation.42.clone.1 | convolution fusion | flops 318832640 | bytes 688128 | tf_op jit(solution)/shard_map/while/body/eval_jaxpr/dot_general | solution.py:33
  337.4 8.9 %fusion.31 = f32[1,2048,128]{2,1,0:T(8,128)S(1)} fusion(f32[2,2048,128]{2,1,0:T(8,128)S(1)} %get-tuple-element.392, bf16[512,2,128]{2,0,1:T(8,128)(2,1)S(1)} %dynamic-slice_bitcast_fusion.2, s32[512]{0:T(512)S(1)} %bitcast.225, s32[512]{0:T(512)S(1)} %bitcast.227, s32[512]{0:T(512)S(1)} %bitcast.229, s32[512]{0:T(512)S(1)} %bitcast.231, ...), kind=kOutput, calls=%fused_computation.38.clone.1 | convolution fusion | flops 319029248 | bytes 2260992 | tf_op jit(solution)/shard_map/while/body/eval_jaxpr/dot_general | solution.py:37
  355.8 9.7 %fusion.32 = bf16[512,1,128]{2,0,1:T(8,128)(2,1)S(1)} fusion(bf16[2,2048,128]{2,1,0:T(8,128)(2,1)} %get-tuple-element.403, s32[512]{0:T(512)S(1)} %bitcast.192, s32[512]{0:T(512)S(1)} %bitcast.194, s32[512]{0:T(512)S(1)} %bitcast.196, s32[512]{0:T(512)S(1)} %bitcast.198, s32[512]{0:T(512)S(1)} %bitcast.200, s32[512]{0:T(512)S(1)} %bitcast.202, ...), kind=kOutput, calls=%fused_computation.43.clone.1 | convolution fusion | flops 318832640 | bytes 688128 | tf_op jit(solution)/shard_map/while/body/eval_jaxpr/dot_general | solution.py:33
  376.1 9.2 %fusion.31 = f32[1,2048,128]{2,1,0:T(8,128)S(1)} fusion(f32[2,2048,128]{2,1,0:T(8,128)S(1)} %get-tuple-element.392, bf16[512,2,128]{2,0,1:T(8,128)(2,1)S(1)} %dynamic-slice_bitcast_fusion.2, s32[512]{0:T(512)S(1)} %bitcast.225, s32[512]{0:T(512)S(1)} %bitcast.227, s32[512]{0:T(512)S(1)} %bitcast.229, s32[512]{0:T(512)S(1)} %bitcast.231, ...), kind=kOutput, calls=%fused_computation.38.clone.1 | convolution fusion | flops 319029248 | bytes 2260992 | tf_op jit(solution)/shard_map/while/body/eval_jaxpr/dot_general | solution.py:37
  413.2 38.3 %all_gather.7 = f32[2,2048]{1,0:T(2,128)S(1)} all-gather(f32[2,256]{1,0:T(2,128)S(1)} %copy-done.2), channel_id=1, replica_groups=mesh['rep'=8,'mod'=32] {'rep'}, dimensions={1}, use_global_device_ids=true | all-gather | bytes 18432 | tf_op jit(solution)/shard_map/all_gather | solution.py:60
  451.5 41.7 %all-reduce.2.cloned.1.call-done = bf16[2,2048,128]{2,1,0:T(8,128)(2,1)} async-done(((bf16[2,2048,128]{2,1,0:T(8,128)(2,1)}), bf16[2,2048,128]{2,1,0:T(8,128)(2,1)}) %all-reduce.2.cloned.1.call-update) | async-done | bytes 1048592 | tf_op jit(solution)/shard_map/psum | solution.py:69
  (121 shorter events, 175.5 us)
Async XLA Ops:
  7.2 20.3 %all-to-all-start = ((s32[128,64,16]{0,2,1:T(8,128)}), s32[128,64,16]{0,2,1:T(8,128)S(1)}, u32[]{:S(2)}, u32[]{:S(2)}) async-start(s32[128,64,16]{0,2,1:T(8,128)} %param.8), calls=%async_computation | async-start | bytes 1048576 | tf_op jit(solution)/shard_map/all_to_all | solution.py:63
  27.4 54.5 %all-to-all-start.1 = ((bf16[128,64,128]{2,0,1:T(8,128)(2,1)}), bf16[128,64,128]{2,0,1:T(8,128)(2,1)S(1)}, u32[]{:S(2)}, u32[]{:S(2)}) async-start(bf16[128,64,128]{2,0,1:T(8,128)(2,1)} %copy.26), calls=%async_computation.1 | async-start | bytes 4194304 | tf_op jit(solution)/shard_map/all_to_all | solution.py:64
  31.4 47.8 %all-gather.2.cloned.1.call-start = ((), (), s32[]{:S(2)}) async-start(), calls=%async_computation.3 | async-start | bytes 2359296 | tf_op jit(solution)/shard_map/all_gather | solution.py:59
  84.0 9.8 %copy-start.1 = (bf16[2,2048,128]{2,1,0:T(8,128)(2,1)S(1)}, bf16[2,2048,128]{2,1,0:T(8,128)(2,1)}, u32[]{:S(2)}) copy-start(bf16[2,2048,128]{2,1,0:T(8,128)(2,1)} %get-tuple-element.403) | copy-start | bytes 3145732 | tf_op jit(solution)/shard_map/while
  123.1 9.8 %copy-start.1 = (bf16[2,2048,128]{2,1,0:T(8,128)(2,1)S(1)}, bf16[2,2048,128]{2,1,0:T(8,128)(2,1)}, u32[]{:S(2)}) copy-start(bf16[2,2048,128]{2,1,0:T(8,128)(2,1)} %get-tuple-element.403) | copy-start | bytes 3145732 | tf_op jit(solution)/shard_map/while
  161.8 9.8 %copy-start.1 = (bf16[2,2048,128]{2,1,0:T(8,128)(2,1)S(1)}, bf16[2,2048,128]{2,1,0:T(8,128)(2,1)}, u32[]{:S(2)}) copy-start(bf16[2,2048,128]{2,1,0:T(8,128)(2,1)} %get-tuple-element.403) | copy-start | bytes 3145732 | tf_op jit(solution)/shard_map/while
  200.7 9.8 %copy-start.1 = (bf16[2,2048,128]{2,1,0:T(8,128)(2,1)S(1)}, bf16[2,2048,128]{2,1,0:T(8,128)(2,1)}, u32[]{:S(2)}) copy-start(bf16[2,2048,128]{2,1,0:T(8,128)(2,1)} %get-tuple-element.403) | copy-start | bytes 3145732 | tf_op jit(solution)/shard_map/while
  239.3 9.8 %copy-start.1 = (bf16[2,2048,128]{2,1,0:T(8,128)(2,1)S(1)}, bf16[2,2048,128]{2,1,0:T(8,128)(2,1)}, u32[]{:S(2)}) copy-start(bf16[2,2048,128]{2,1,0:T(8,128)(2,1)} %get-tuple-element.403) | copy-start | bytes 3145732 | tf_op jit(solution)/shard_map/while
  278.2 9.8 %copy-start.1 = (bf16[2,2048,128]{2,1,0:T(8,128)(2,1)S(1)}, bf16[2,2048,128]{2,1,0:T(8,128)(2,1)}, u32[]{:S(2)}) copy-start(bf16[2,2048,128]{2,1,0:T(8,128)(2,1)} %get-tuple-element.403) | copy-start | bytes 3145732 | tf_op jit(solution)/shard_map/while
  316.9 9.8 %copy-start.1 = (bf16[2,2048,128]{2,1,0:T(8,128)(2,1)S(1)}, bf16[2,2048,128]{2,1,0:T(8,128)(2,1)}, u32[]{:S(2)}) copy-start(bf16[2,2048,128]{2,1,0:T(8,128)(2,1)} %get-tuple-element.403) | copy-start | bytes 3145732 | tf_op jit(solution)/shard_map/while
  355.8 9.8 %copy-start.1 = (bf16[2,2048,128]{2,1,0:T(8,128)(2,1)S(1)}, bf16[2,2048,128]{2,1,0:T(8,128)(2,1)}, u32[]{:S(2)}) copy-start(bf16[2,2048,128]{2,1,0:T(8,128)(2,1)} %get-tuple-element.403) | copy-start | bytes 3145732 | tf_op jit(solution)/shard_map/while
  404.0 94.4 %all-to-all-start.2 = ((bf16[4096,2,128]{2,1,0:T(2,128)(2,1)}), bf16[4096,2,128]{2,1,0:T(2,128)(2,1)}, u32[]{:S(2)}, u32[]{:S(2)}) async-start(bf16[4096,2,128]{2,1,0:T(2,128)(2,1)} %copy.31), calls=%async_computation.2 | async-start | bytes 4194304 | tf_op jit(solution)/shard_map/all_to_all | solution.py:66
  412.0 81.2 %all-reduce.2.cloned.1.call-start = ((), (), s32[]{:S(2)}) async-start(), calls=%async_computation.4 | async-start | bytes 2097152 | tf_op jit(solution)/shard_map/psum | solution.py:69
  412.0 1.1 copy-start.2
  413.1 82.5 %copy-start = (f32[2,2048,128]{2,1,0:T(8,128)S(1)}, f32[2,2048,128]{2,1,0:T(8,128)}, u32[]{:S(2)}) copy-start(f32[2,2048,128]{2,1,0:T(8,128)} %all-gather.2.cloned.1.call-done) | copy-start | bytes 6291460
Sparse Core Ops, SparseCore 0:
  34.1 45.0 all-gather.1
  416.0 77.1 all-reduce.1
where the time goes:
time: 515 us; the launch traced here: 510 us
  matrix products  291 us (57%)
  waiting for transfers between devices  95.8 us (19%)
  blocking collectives  38.3 us (7%)
  local copies, waits for them, and re-layouts  25.8 us (5%)
  starting transfers between devices  21.3 us (4%)
  other arithmetic  16.1 us (3%)
  between operations  14.4 us (3%)
  loops' own time  7.22 us (1%)
    dot_general x16, matrix products, step(): jnp.dot(counts_low, lookup[owned_index], preferred_element_type=jnp.float32)  149 us
    dot_general x16, matrix products, step(): lax.dot_general(counts_low, cot_blk[:, owned_index, :], (((0,), (0,)), ((...  142 us
    all_gather x1, waiting for transfers between devices, local(): lax.all_gather(table, 'rep', axis=1, tiled=True)  46.6 us
    psum x1, waiting for transfers between devices, local(): total = lax.psum(row_grad.astype(jnp.bfloat16), 'rep').astype(jnp.float32)  41.7 us
    all_gather x1, blocking collectives, local(): lax.all_gather(accum, 'rep', axis=1, tiled=True)  38.3 us
  transfers between devices with their start and end apart: 5, of which 3 were waited for; matrix products, arithmetic and copies ran while one was open for 3% of the time, Pallas kernels for 0%

commit v1 on v0

v1 whole, which is shorter than its diff:
```python
import functools

import jax
import jax.numpy as jnp
from jax import lax
from jax.experimental import pallas as pl
from jax.experimental.pallas import tpu as pltpu
from jax.sharding import PartitionSpec as P

BF16, F32 = jnp.bfloat16, jnp.float32
SUB = 8
HIGH = 8


def pool_kernel(blocks, unroll, ids_ref, cot_ref, table_ref, pooled_ref, grad_ref, high_key, low_key, counts, total):
    rows = table_ref.shape[1]
    low = rows // HIGH
    pair_rows = 2 * SUB
    step = pl.program_id(0)
    ids = ids_ref[...]
    lane = lax.broadcasted_iota(jnp.int32, ids.shape, 1)
    high_key[...] = ((ids // low) * pair_rows + lane // (256 // pair_rows)).astype(F32)
    low_key[...] = (ids % low).astype(F32)
    iota = lax.broadcasted_iota(jnp.int32, (pair_rows, 256), 0).astype(F32)
    one, zero = jnp.ones((pair_rows, 256), BF16), jnp.zeros((pair_rows, 256), BF16)

    def count_block(b, _):
        high_row = jnp.broadcast_to(high_key[pl.ds(b, 1), :], (pair_rows, 256)).astype(BF16)
        low_row = jnp.broadcast_to(low_key[pl.ds(b, 1), :], (pair_rows, 256)).astype(BF16)
        high_hot = jnp.concatenate(
            [jnp.where(high_row == (iota + pair_rows * i).astype(BF16), one, zero) for i in range(HIGH)], 0
        )
        low_hot = jnp.concatenate(
            [jnp.where(low_row == (iota + pair_rows * i).astype(BF16), one, zero) for i in range(low // pair_rows)], 0
        )
        out = lax.dot_general(high_hot, low_hot, (((1,), (1,)), ((), ())), preferred_element_type=F32).astype(BF16)
        at = pl.multiple_of(b * pair_rows, pair_rows)
        for i in range(HIGH):
            counts[pl.ds(at, pair_rows), i * low : (i + 1) * low] = out[i * pair_rows : (i + 1) * pair_rows]
        return 0

    lax.fori_loop(0, blocks, count_block, 0, unroll=unroll)
    both = jnp.concatenate([table_ref[0], table_ref[1]], 1)
    sums = jnp.dot(counts[...], both, preferred_element_type=F32)
    parity = lax.broadcasted_iota(jnp.int32, (blocks * pair_rows, 128), 0) % 2
    pooled_ref[...] = jnp.where(parity == 0, sums[:, :128], sums[:, 128:]).astype(BF16)
    cot = cot_ref[...]
    second = cot * parity.astype(F32).astype(BF16)
    split = jnp.concatenate([cot - second, second], 1)
    grad = lax.dot_general(split, counts[...], (((0,), (0,)), ((), ())), preferred_element_type=F32)

    @pl.when(step == 0)
    def _():
        total[...] = grad

    @pl.when(step > 0)
    def _():
        total[...] += grad

    @pl.when(step == pl.num_programs(0) - 1)
    def _():
        grad_ref[0] = total[:128].T.astype(BF16)
        grad_ref[1] = total[128:].T.astype(BF16)


def pool_and_grad(ids, cot, lookup, blocks=64, unroll=16):
    all_blocks, rows = ids.shape[0], lookup.shape[1]
    height = blocks * 2 * SUB
    return pl.pallas_call(
        functools.partial(pool_kernel, blocks, unroll),
        grid=(all_blocks // blocks,),
        out_shape=[
            jax.ShapeDtypeStruct((all_blocks * 2 * SUB, 128), BF16),
            jax.ShapeDtypeStruct((2, rows, 128), BF16),
        ],
        in_specs=[
            pl.BlockSpec((blocks, 256), lambda i: (i, 0)),
            pl.BlockSpec((height, 128), lambda i: (i, 0)),
            pl.BlockSpec((2, rows, 128), lambda i: (0, 0, 0)),
        ],
        out_specs=[
            pl.BlockSpec((height, 128), lambda i: (i, 0)),
            pl.BlockSpec((2, rows, 128), lambda i: (0, 0, 0)),
        ],
        scratch_shapes=[
            pltpu.VMEM((blocks, 256), F32),
            pltpu.VMEM((blocks, 256), F32),
            pltpu.VMEM((height, rows), BF16),
            pltpu.VMEM((256, rows), F32),
        ],
        compiler_params=pltpu.CompilerParams(vmem_limit_bytes=48 << 20),
        name="pool_and_grad",
    )(ids, cot, lookup)


def adagrad(weights, sums, grad):
    new_sums = sums + jnp.mean(grad * grad, axis=-1)
    new_weights = weights - 0.1 * grad / jnp.sqrt(new_sums)[:, :, None]
    return (new_weights, new_sums)


def local(table, accum, bag_rows, pooled_grad):
    samples, tables, pool_len = bag_rows.shape
    pairs = tables // 2
    ids = bag_rows.astype(jnp.int16).reshape(samples // SUB, SUB, pairs, 2, pool_len)
    ids = ids.transpose(2, 0, 1, 3, 4).reshape(pairs, samples // SUB, SUB * 2 * pool_len)
    group_ids = lax.all_to_all(ids, "mod", split_axis=0, concat_axis=0, tiled=True)
    cot = pooled_grad.reshape(samples, pairs, 2, 128).transpose(1, 0, 2, 3).reshape(pairs, samples * 2, 128)
    group_cot = lax.all_to_all(cot, "mod", split_axis=0, concat_axis=0, tiled=True)
    full_accum = lax.all_gather(accum, "rep", axis=1, tiled=True)
    full_table = lax.all_gather(table, "rep", axis=1, tiled=True)
    pooled_group, row_grad = pool_and_grad(
        group_ids.reshape(-1, 256).astype(jnp.int32), group_cot.reshape(-1, 128), full_table.astype(BF16)
    )
    pooled = lax.all_to_all(pooled_group.reshape(pairs, samples * 2, 128), "mod", split_axis=0, concat_axis=0, tiled=True)
    pooled = pooled.reshape(pairs, samples, 2, 128).transpose(1, 0, 2, 3).reshape(samples, tables, 128)
    total = lax.psum(row_grad, "rep").astype(F32)
    new_table, new_accum = adagrad(full_table, full_accum, total)
    return (pooled, new_table, new_accum)


def solution(mesh):
    in_specs = (
        P("mod", "rep", None),
        P("mod", "rep"),
        P(("rep", "mod"), None, None),
        P(("rep", "mod"), None, None),
    )
    out_specs = (P(("rep", "mod"), None, None), P("mod", None, None), P("mod", None))
    return jax.shard_map(local, mesh=mesh, in_specs=in_specs, out_specs=out_specs, check_vma=False)
```

time: 515 us -> 245 us (0.48)
  matrix products: 291 us -> 0 us
  Pallas kernels: 0 us -> 49.9 us
  other arithmetic: 16.1 us -> 8.07 us
  local copies, waits for them, and re-layouts: 25.8 us -> 17.9 us
  loops' own time: 7.22 us -> 0 us
    dot_general x32 -> x0, matrix products: 291 us -> none  [the longest x16 149 us: step(): jnp.dot(counts_low, lookup[owned_index], preferred_element_type=jnp.float32)]
    pallas_call x0 -> x1, Pallas kernels: none -> 49.9 us  [pool_and_grad(): pl.pallas_call(functools.partial(pool_kernel, blocks, unroll), grid=(all_...]
    transpose x0 -> x2, local copies, waits for them, and re-layouts: none -> 8.13 us  [the longest x1 5.09 us: local(): pooled_grad.reshape(samples, pairs, 2, 128).transpose(1, 0, 2, 3)]
    squeeze x16 -> x0, local copies, waits for them, and re-layouts: 7.8 us -> none  [the longest x8 7.74 us: pool_and_grad(): row_grad, pooled_blocks = lax.scan(step, start, (ids_blocks, cot_blocks))]
    another operation x1 -> x0, loops' own time: 7.22 us -> none  [pool_and_grad(): row_grad, pooled_blocks = lax.scan(step, start, (ids_blocks, cot_blocks))]
    dynamic_update_slice x8 -> x0, other arithmetic: 6.03 us -> none  [pool_and_grad(): row_grad, pooled_blocks = lax.scan(step, start, (ids_blocks, cot_blocks))]
    unnamed x6, local copies, waits for them, and re-layouts: 6.95 us -> 1.33 us
  transfers between devices with their start and end apart: 5 -> 5, of which waited for: 3 -> 3; matrix products, arithmetic and copies ran while one was open for 3% -> 5% of each run, Pallas kernels for 0% -> 0%
where the time goes in v1:
time: 245 us; the launch traced here: 244 us
  waiting for transfers between devices  93.1 us (38%)
  Pallas kernels  49.9 us (20%)
  blocking collectives  39.2 us (16%)
  starting transfers between devices  22 us (9%)
  local copies, waits for them, and re-layouts  17.9 us (7%)
  between operations  14.1 us (6%)
  other arithmetic  8.07 us (3%)
    pallas_call x1, Pallas kernels, pool_and_grad(): pl.pallas_call(functools.partial(pool_kernel, blocks, unroll), grid=(all_...  49.9 us
    all_gather x1, waiting for transfers between devices, local(): full_table = lax.all_gather(table, 'rep', axis=1, tiled=True)  46.8 us
    psum x1, waiting for transfers between devices, local(): total = lax.psum(row_grad, 'rep').astype(F32)  41.4 us
    all_gather x1, blocking collectives, local(): full_accum = lax.all_gather(accum, 'rep', axis=1, tiled=True)  39.2 us
    all_to_all x1, starting transfers between devices, local(): lax.all_to_all(ids, 'mod', split_axis=0, concat_axis=0, tiled=True)  9.22 us
    all_to_all x1, starting transfers between devices, local(): lax.all_to_all(pooled_group.reshape(pairs, samples * 2, 128), 'mod', spli...  7.89 us
    reshape x1, local copies, waits for them, and re-layouts, local(): pooled.reshape(pairs, samples, 2, 128).transpose(1, 0, 2, 3)  5.28 us
    transpose x1, local copies, waits for them, and re-layouts, local(): pooled_grad.reshape(samples, pairs, 2, 128).transpose(1, 0, 2, 3)  5.09 us
  transfers between devices with their start and end apart: 5, of which 3 were waited for; matrix products, arithmetic and copies ran while one was open for 5% of the time, Pallas kernels for 0%

profile of v1, /device:TPU:1, one launch (start us, length us, event | category | flops | bytes accessed | tf_op | source)
XLA Modules:
  0.0 244.2 jit_solution(14377164636408288530)
XLA Ops:
  7.2 1.1 convert_element_type.14
  8.2 1.7 copy.15
  9.9 3.0 %copy.16 = s16[32,16,8,2,16]{0,4,3,2,1:T(8,128)(2,1)S(1)} copy(s16[32,16,8,2,16]{4,2,1,3,0:T(8,128)(2,1)S(1)} %bitcast.18) | data formatting | bytes 524288 | tf_op jit(solution)/shard_map/transpose | solution.py:106
  13.0 1.4 copy.17
  14.4 9.2 %all-to-all-start = ((s16[32,16,256]{2,1,0:T(8,128)(2,1)}), s16[32,16,256]{2,1,0:T(8,128)(2,1)S(1)}, u32[]{:S(2)}, u32[]{:S(2)}) async-start(s16[32,16,256]{2,1,0:T(8,128)(2,1)} %copy.17), calls=%async_computation | async-start | bytes 524288 | tf_op jit(solution)/shard_map/all_to_all | solution.py:107
  23.7 5.1 %copy.18 = bf16[32,128,2,128]{3,2,1,0:T(2,128)(2,1)} copy(bf16[32,128,2,128]{3,2,0,1:T(2,128)(2,1)} %bitcast.20) | data formatting | bytes 4194304 | tf_op jit(solution)/shard_map/transpose | solution.py:108
  28.8 3.5 %all-to-all-done = s16[32,16,256]{2,1,0:T(8,128)(2,1)S(1)} async-done(((s16[32,16,256]{2,1,0:T(8,128)(2,1)}), s16[32,16,256]{2,1,0:T(8,128)(2,1)S(1)}, u32[]{:S(2)}, u32[]{:S(2)}) %all-to-all-start) | async-done | bytes 262176 | tf_op jit(solution)/shard_map/all_to_all | solution.py:107
  32.2 4.8 %all-to-all-start.1 = ((bf16[32,256,128]{2,1,0:T(8,128)(2,1)}), bf16[32,256,128]{2,1,0:T(8,128)(2,1)}, u32[]{:S(2)}, u32[]{:S(2)}) async-start(bf16[32,256,128]{2,1,0:T(8,128)(2,1)} %bitcast.6), calls=%async_computation.1 | async-start | bytes 4194304 | tf_op jit(solution)/shard_map/all_to_all | solution.py:109
  37.0 0.0 all-gather.2.cloned.1.call-start
  37.0 0.7 all-gather.2.cloned.1.call-update
  37.7 0.1 bitcast_convert_fusion.ids_ref
  37.8 46.8 %all-gather.2.cloned.1.call-done = f32[2,2048,128]{2,1,0:T(8,128)} async-done(((f32[2,256,128]{2,1,0:T(8,128)}), f32[2,2048,128]{2,1,0:T(8,128)}) %all-gather.2.cloned.1.call-update) | async-done | bytes 2097168 | tf_op jit(solution)/shard_map/all_gather | solution.py:111
  84.6 1.7 convert_element_type.17.table_ref
  86.3 49.9 %pool_and_grad.1 = (bf16[8192,128]{1,0:T(8,128)(2,1)S(1)}, bf16[2,2048,128]{2,1,0:T(8,128)(2,1)}) custom-call(s32[512,256]{1,0:T(8,128)S(1)} %bitcast_convert_fusion.ids_ref, bf16[8192,128]{1,0:T(8,128)(2,1)} %bitcast.7.cot_ref, bf16[2,2048,128]{2,1,0:T(8,128)(2,1)S(1)} %convert_element_type.17.table_ref), custom_call_target="tpu_custom_call" | custom-call | tf_op jit(solution)/shard_map/pool_and_grad/pallas_call | solution.py:69
  136.3 1.3 copy-done
  137.6 7.9 %all-to-all-start.2 = ((bf16[32,256,128]{2,1,0:T(8,128)(2,1)}), bf16[32,256,128]{2,1,0:T(8,128)(2,1)}, u32[]{:S(2)}, u32[]{:S(2)}) async-start(bf16[32,256,128]{2,1,0:T(8,128)(2,1)} %bitcast.17), calls=%async_computation.2 | async-start | bytes 4194304 | tf_op jit(solution)/shard_map/all_to_all | solution.py:115
  145.5 0.0 all-reduce.2.cloned.1.call-start
  145.6 0.7 all-reduce.2.cloned.1.call-update
  146.3 39.2 %all_gather.7 = f32[2,2048]{1,0:T(2,128)S(1)} all-gather(f32[2,256]{1,0:T(2,128)S(1)} %copy-done.2), channel_id=1, replica_groups=mesh['rep'=8,'mod'=32] {'rep'}, dimensions={1}, use_global_device_ids=true | all-gather | bytes 18432 | tf_op jit(solution)/shard_map/all_gather | solution.py:110
  185.4 41.4 %all-reduce.2.cloned.1.call-done = bf16[2,2048,128]{2,1,0:T(8,128)(2,1)} async-done(((bf16[2,2048,128]{2,1,0:T(8,128)(2,1)}), bf16[2,2048,128]{2,1,0:T(8,128)(2,1)}) %all-reduce.2.cloned.1.call-update) | async-done | bytes 1048592 | tf_op jit(solution)/shard_map/psum | solution.py:117
  226.9 1.8 fusion.2
  228.7 0.6 fusion.3
  229.3 2.7 %fusion.1 = f32[2,2048,128]{2,1,0:T(8,128)} fusion(f32[2,2048,128]{2,1,0:T(8,128)S(1)} %copy-done.1, bf16[2,2048,128]{2,1,0:T(8,128)(2,1)} %all-reduce.2.cloned.1.call-done, f32[2,2048]{1,0:T(2,128)S(1)} %get-tuple-element.7), kind=kLoop, calls=%fused_computation.3 | loop fusion | flops 2097152 | bytes 5259264 | tf_op jit(solution)/shard_map/sub | solution.py:98
  232.1 5.3 %copy.19 = bf16[32,128,2,128]{3,2,0,1:T(2,128)(2,1)} copy(bf16[32,128,2,128]{3,2,1,0:T(2,128)(2,1)} %bitcast.9) | data formatting | bytes 4194304 | tf_op jit(solution)/shard_map/reshape | solution.py:116
  (7 shorter events, 0.0 us)
Async XLA Ops:
  14.4 17.8 %all-to-all-start = ((s16[32,16,256]{2,1,0:T(8,128)(2,1)}), s16[32,16,256]{2,1,0:T(8,128)(2,1)S(1)}, u32[]{:S(2)}, u32[]{:S(2)}) async-start(s16[32,16,256]{2,1,0:T(8,128)(2,1)} %copy.17), calls=%async_computation | async-start | bytes 524288 | tf_op jit(solution)/shard_map/all_to_all | solution.py:107
  32.2 54.1 %all-to-all-start.1 = ((bf16[32,256,128]{2,1,0:T(8,128)(2,1)}), bf16[32,256,128]{2,1,0:T(8,128)(2,1)}, u32[]{:S(2)}, u32[]{:S(2)}) async-start(bf16[32,256,128]{2,1,0:T(8,128)(2,1)} %bitcast.6), calls=%async_computation.1 | async-start | bytes 4194304 | tf_op jit(solution)/shard_map/all_to_all | solution.py:109
  37.0 47.6 %all-gather.2.cloned.1.call-start = ((), (), s32[]{:S(2)}) async-start(), calls=%async_computation.3 | async-start | bytes 2359296 | tf_op jit(solution)/shard_map/all_gather | solution.py:111
  136.3 1.3 copy-start
  137.6 8.7 %copy-start.2 = (f32[2,256]{1,0:T(2,128)S(1)}, f32[2,256]{1,0:T(2,128)}, u32[]{:S(2)}) copy-start(f32[2,256]{1,0:T(2,128)} %param.5) | copy-start | bytes 6148
  137.6 94.5 %all-to-all-start.2 = ((bf16[32,256,128]{2,1,0:T(8,128)(2,1)}), bf16[32,256,128]{2,1,0:T(8,128)(2,1)}, u32[]{:S(2)}, u32[]{:S(2)}) async-start(bf16[32,256,128]{2,1,0:T(8,128)(2,1)} %bitcast.17), calls=%async_computation.2 | async-start | bytes 4194304 | tf_op jit(solution)/shard_map/all_to_all | solution.py:115
  145.5 83.8 %copy-start.1 = (f32[2,2048,128]{2,1,0:T(8,128)S(1)}, f32[2,2048,128]{2,1,0:T(8,128)}, u32[]{:S(2)}) copy-start(f32[2,2048,128]{2,1,0:T(8,128)} %all-gather.2.cloned.1.call-done) | copy-start | bytes 6291460
  145.5 81.3 %all-reduce.2.cloned.1.call-start = ((), (), s32[]{:S(2)}) async-start(), calls=%async_computation.4 | async-start | bytes 2097152 | tf_op jit(solution)/shard_map/psum | solution.py:117
Sparse Core Ops, SparseCore 0:
  39.7 44.8 all-gather.1
  149.6 77.2 all-reduce.1

commit v2 on v0

v2 whole, which is shorter than its diff:
```python
import functools

import jax
import jax.numpy as jnp
from jax import lax
from jax.experimental import pallas as pl
from jax.experimental.pallas import tpu as pltpu
from jax.sharding import PartitionSpec as P

BF16, F32, I32 = jnp.bfloat16, jnp.float32, jnp.int32
SUB = 8
HIGH = 8
LOW = 256
PEERS = 32
CHUNK = 256
BATCHED = 4
GROUPS = PEERS // BATCHED
LAG = 2
STRIDE = 11
MESH = pl.DeviceIdType.MESH


def away(me, step, sign):
    x, y, z = me // 8, (me // 2) % 4, me % 2
    dx, dy, dz = step // 8, (step // 2) % 4, step % 2
    return ((x + sign * dx + 4) % 4) * 8 + ((y + sign * dy + 4) % 4) * 2 + (z + dz) % 2


def order(i):
    return (i * STRIDE) % PEERS


def step_kernel(
    ids_ref, cot_ref, table_ref, accum_ref, pooled_ref, new_table_ref, new_accum_ref,
    ids_buf, cot_buf, pooled_buf, shards, both, high_key, low_key, counts, split,
    pair_out, pair_in, ring_out, ring_in, own_grad, new_shard, new_sums,
    ids_out, ids_in, cot_out, cot_in, pool_out, pool_in, local_sem,
    tab_out, tab_in, tab_fwd_out, tab_fwd_in, px_out, px_in, rs_out, rs_in,
    new_out, new_in, fwd_out, fwd_in, acc_out, acc_in,
):
    me = lax.axis_index("mod")
    rep = lax.axis_index("rep")
    high, core = rep // 2, rep % 2
    twin = {"rep": high * 2 + 1 - core}

    def ring(step):
        return {"rep": ((high + step + 4) % 4) * 2 + core}

    def remote(src, dst, out_sem, in_sem, device):
        return pltpu.make_async_remote_copy(
            src_ref=src, dst_ref=dst, send_sem=out_sem, recv_sem=in_sem, device_id=device, device_id_type=MESH
        )

    def ids_copy(k):
        return remote(ids_ref.at[away(me, k, 1)], ids_buf.at[k], ids_out.at[k], ids_in.at[k], {"mod": away(me, k, 1)})

    def cot_copy(k):
        return remote(cot_ref.at[:, away(me, k, 1)], cot_buf.at[k], cot_out.at[k], cot_in.at[k], {"mod": away(me, k, 1)})

    def pool_copy(k):
        return remote(pooled_buf.at[k], pooled_ref.at[:, me], pool_out.at[k], pool_in.at[k], {"mod": away(me, k, -1)})

    def pool_arrival(k):
        return remote(
            pooled_buf.at[k], pooled_ref.at[:, away(me, k, 1)], pool_out.at[k], pool_in.at[k], {"mod": away(me, k, -1)}
        )

    def shard_copy(step, device, out_sem, in_sem, offset=0):
        at = ((high + offset + 4) % 4) * 2 + core
        return remote(shards.at[at], shards.at[at], out_sem.at[step], in_sem.at[step], device)

    barrier = pltpu.get_barrier_semaphore()

    @pl.loop(1, PEERS)
    def _(k):
        pl.semaphore_signal(barrier, inc=1, device_id={"mod": away(me, k, 1)}, device_id_type=MESH)

    @pl.loop(0, 8)
    def _(r):
        @pl.when(r != rep)
        def _():
            pl.semaphore_signal(barrier, inc=1, device_id={"rep": r}, device_id_type=MESH)

    own_ids = pltpu.make_async_copy(ids_ref.at[me], ids_buf.at[0], local_sem.at[0])
    own_cot = pltpu.make_async_copy(cot_ref.at[:, me], cot_buf.at[0], local_sem.at[1])
    own_ids.start()
    own_cot.start()
    shards[rep] = table_ref[...].astype(BF16)
    pl.semaphore_wait(barrier, PEERS - 1 + 7)

    @pl.loop(1, PEERS)
    def _(i):
        ids_copy(order(i)).start()

    for step in (1, 3, 2):
        shard_copy(step, ring(step), tab_out, tab_in).start()
    shard_copy(0, twin, tab_fwd_out, tab_fwd_in).start()

    @pl.loop(1, PEERS)
    def _(i):
        cot_copy(order(i)).start()

    own_ids.wait()
    own_cot.wait()

    lane = lax.broadcasted_iota(I32, (16, 256), 1)
    iota = lax.broadcasted_iota(I32, (16, 256), 0).astype(F32)
    one, zero = jnp.ones((16, 256), BF16), jnp.zeros((16, 256), BF16)
    sample3 = lax.broadcasted_iota(I32, (16, SUB, 128), 1)
    lane3 = lax.broadcasted_iota(I32, (16, SUB, 128), 2) // 32

    def count_chunk(i):
        k = order(i)

        @pl.when(i > 0)
        def _():
            ids_copy(k).wait_recv()

        ids = ids_buf[k].astype(I32).astype(F32)
        turned = jnp.concatenate([ids] * 4, 0).T.reshape(16, SUB, 128)
        first = jnp.sum(jnp.where(sample3 == lane3, turned, 0.0), axis=1)
        second = jnp.sum(jnp.where(sample3 == lane3 + 4, turned, 0.0), axis=1)
        flat = jnp.concatenate([first, second], 1).astype(I32)
        high_key[...] = ((flat // LOW) * 16 + lane // 16).astype(F32)
        low_key[...] = (flat % LOW).astype(F32)
        base = pl.multiple_of(i * CHUNK, CHUNK)
        for b in range(16):
            high_row = jnp.broadcast_to(high_key[b : b + 1, :], (16, 256)).astype(BF16)
            low_row = jnp.broadcast_to(low_key[b : b + 1, :], (16, 256)).astype(BF16)
            high_hot = jnp.concatenate(
                [jnp.where(high_row == (iota + 16 * j).astype(BF16), one, zero) for j in range(HIGH)], 0
            )
            low_hot = jnp.concatenate(
                [jnp.where(low_row == (iota + 16 * j).astype(BF16), one, zero) for j in range(LOW // 16)], 0
            )
            out = lax.dot_general(high_hot, low_hot, (((1,), (1,)), ((), ())), preferred_element_type=F32).astype(BF16)
            for j in range(HIGH):
                counts[j, pl.ds(base + b * 16, 16), :] = out[j * 16 : (j + 1) * 16]

    parity = lax.broadcasted_iota(I32, (BATCHED * CHUNK, 128), 0) % 2
    odd = (lax.broadcasted_iota(I32, (128, CHUNK), 1) % 2).astype(F32).astype(BF16)

    def pool_group(g):
        base = pl.multiple_of(g * BATCHED * CHUNK, BATCHED * CHUNK)
        rows = jnp.concatenate([counts[j, pl.ds(base, BATCHED * CHUNK), :] for j in range(HIGH)], 1)
        sums = jnp.dot(rows, both[...], preferred_element_type=F32)
        picked = jnp.where(parity == 0, sums[:, :128], sums[:, 128:]).astype(BF16)
        for b in range(BATCHED):
            pooled_buf[order(g * BATCHED + b)] = picked[b * CHUNK : (b + 1) * CHUNK].reshape(CHUNK // 2, 2, 128)
        for b in range(BATCHED):
            i = g * BATCHED + b

            @pl.when(i > 0)
            def _(i=i):
                pool_copy(order(i)).start()

    def turn_cotangents(g):
        @pl.loop(0, BATCHED)
        def _(b):
            i = g * BATCHED + b
            k = order(i)

            @pl.when(i > 0)
            def _():
                cot_copy(k).wait_recv()

            turned = cot_buf[k].reshape(CHUNK, 128).T
            at = pl.ds(pl.multiple_of(i * CHUNK, CHUNK), CHUNK)
            second = turned * odd
            split[0:128, at] = turned - second
            split[128:256, at] = second

    @pl.loop(0, GROUPS + LAG)
    def _(g):
        @pl.when(g < GROUPS)
        def _():
            @pl.loop(0, BATCHED)
            def _(b):
                count_chunk(g * BATCHED + b)

        @pl.when(g == 0)
        def _():
            for step in (1, 3, 2):
                shard_copy(step, ring(step), tab_out, tab_in, -step).wait_recv()
                shard_copy(step, twin, tab_fwd_out, tab_fwd_in, -step).start()

        @pl.when(g == LAG)
        def _():
            for step in range(4):
                at = ((high - step + 4) % 4) * 2 + 1 - core
                remote(shards.at[at], shards.at[at], tab_fwd_out.at[step], tab_fwd_in.at[step], twin).wait_recv()
            for j in range(HIGH):
                both[j * LOW : (j + 1) * LOW, :] = jnp.concatenate([shards[j, 0], shards[j, 1]], 1)

        @pl.when(g >= LAG)
        def _():
            pool_group(g - LAG)
            turn_cotangents(g - LAG)

    own_pool = pltpu.make_async_copy(pooled_buf.at[0], pooled_ref.at[:, me], local_sem.at[2])
    own_pool.start()

    def grad_block(at):
        return jnp.dot(split[...], counts[at], preferred_element_type=F32)

    def pair_copy(step):
        return remote(pair_out.at[step], pair_in.at[step], px_out.at[step], px_in.at[step], twin)

    def ring_copy(step):
        return remote(ring_out.at[step], ring_in.at[step], rs_out.at[step], rs_in.at[step], ring(step))

    @pl.loop(1, 5)
    def _(n):
        step = n % 4
        pair_out[step] = grad_block(((high + step) % 4) * 2 + 1 - core).astype(BF16)
        pair_copy(step).start()

    @pl.loop(1, 5)
    def _(n):
        step = n % 4
        own = grad_block(((high + step) % 4) * 2 + core)
        pair_copy(step).wait_recv()
        total = own + pair_in[step].astype(F32)

        @pl.when(step > 0)
        def _():
            ring_out[step] = total.astype(BF16)
            ring_copy(step).start()

        @pl.when(step == 0)
        def _():
            own_grad[...] = total

    for step in (1, 2, 3):
        ring_copy(step).wait_recv()
    grad = own_grad[...] + ring_in[1].astype(F32) + ring_in[2].astype(F32) + ring_in[3].astype(F32)
    for t in range(2):
        one_grad = grad[t * 128 : (t + 1) * 128]
        sums = accum_ref[t : t + 1, :] + jnp.mean(one_grad * one_grad, axis=0, keepdims=True)
        new_sums[t : t + 1, :] = sums
        new_shard[t] = table_ref[t] - (0.1 * one_grad / jnp.sqrt(sums)).T

    here = pl.ds(pl.multiple_of(rep * LOW, LOW), LOW)
    own_new = pltpu.make_async_copy(new_shard, new_table_ref.at[:, rep], local_sem.at[3])
    own_sums = pltpu.make_async_copy(new_sums, new_accum_ref.at[:, here], local_sem.at[4])

    def new_copy(step, device):
        return remote(new_shard, new_table_ref.at[:, rep], new_out.at[step], new_in.at[step], device)

    def new_arrival(step, device):
        at = ((high - step + 4) % 4) * 2 + core
        return remote(new_shard, new_table_ref.at[:, at], new_out.at[step], new_in.at[step], device)

    def new_forward(step):
        at = ((high - step + 4) % 4) * 2 + core
        return remote(new_table_ref.at[:, at], new_table_ref.at[:, at], fwd_out.at[step], fwd_in.at[step], twin)

    def sums_copy(r, at):
        where = pl.ds(pl.multiple_of(at * LOW, LOW), LOW)
        return remote(new_sums, new_accum_ref.at[:, where], acc_out.at[r], acc_in.at[r], {"rep": (rep + r) % 8})

    for step in (1, 3, 2):
        new_copy(step, ring(step)).start()
    new_twin = remote(new_shard, new_table_ref.at[:, rep], fwd_out.at[0], fwd_in.at[0], twin)
    new_twin.start()

    @pl.loop(1, 8)
    def _(r):
        sums_copy(r, rep).start()

    own_new.start()
    own_sums.start()
    for step in (1, 3, 2):
        new_arrival(step, ring(step)).wait_recv()
        new_forward(step).start()
    for step in range(4):
        at = ((high - step + 4) % 4) * 2 + 1 - core
        remote(new_table_ref.at[:, at], new_table_ref.at[:, at], fwd_out.at[step], fwd_in.at[step], twin).wait_recv()

    @pl.loop(1, 8)
    def _(r):
        sums_copy(r, (rep - r + 8) % 8).wait_recv()

    @pl.loop(1, PEERS)
    def _(k):
        pool_arrival(k).wait_recv()

    own_pool.wait()
    own_new.wait()
    own_sums.wait()

    @pl.loop(1, PEERS)
    def _(k):
        ids_copy(k).wait_send()
        cot_copy(k).wait_send()
        pool_copy(k).wait_send()

    for step in (1, 2, 3):
        shard_copy(step, ring(step), tab_out, tab_in).wait_send()
        shard_copy(step, twin, tab_fwd_out, tab_fwd_in, -step).wait_send()
        ring_copy(step).wait_send()
        new_copy(step, ring(step)).wait_send()
        new_forward(step).wait_send()
    shard_copy(0, twin, tab_fwd_out, tab_fwd_in).wait_send()
    new_twin.wait_send()
    for step in range(4):
        pair_copy(step).wait_send()

    @pl.loop(1, 8)
    def _(r):
        sums_copy(r, rep).wait_send()


def local(table, accum, bag_rows, pooled_grad):
    samples, tables, pool_len = bag_rows.shape
    pairs = tables // 2
    ids = bag_rows.transpose(1, 2, 0).astype(jnp.int16).reshape(pairs, 2 * pool_len, samples)
    cot = pooled_grad.reshape(samples, pairs, 2, 128)
    rows = PEERS * CHUNK
    dma = pltpu.SemaphoreType.DMA
    pooled, new_table, new_accum = pl.pallas_call(
        step_kernel,
        out_shape=[
            jax.ShapeDtypeStruct((samples, pairs, 2, 128), BF16),
            jax.ShapeDtypeStruct((2, 8, LOW, 128), F32),
            jax.ShapeDtypeStruct((2, 8 * LOW), F32),
        ],
        in_specs=[
            pl.BlockSpec(memory_space=pl.ANY),
            pl.BlockSpec(memory_space=pl.ANY),
            pl.BlockSpec(memory_space=pltpu.VMEM),
            pl.BlockSpec(memory_space=pltpu.VMEM),
        ],
        out_specs=[pl.BlockSpec(memory_space=pl.ANY)] * 3,
        scratch_shapes=[
            pltpu.VMEM((PEERS, 32, 128), jnp.int16),
            pltpu.VMEM((PEERS, CHUNK // 2, 2, 128), BF16),
            pltpu.VMEM((PEERS, CHUNK // 2, 2, 128), BF16),
            pltpu.VMEM((8, 2, LOW, 128), BF16),
            pltpu.VMEM((HIGH * LOW, 256), BF16),
            pltpu.VMEM((16, 256), F32),
            pltpu.VMEM((16, 256), F32),
            pltpu.VMEM((HIGH, rows, LOW), BF16),
            pltpu.VMEM((256, rows), BF16),
            pltpu.VMEM((4, 256, LOW), BF16),
            pltpu.VMEM((4, 256, LOW), BF16),
            pltpu.VMEM((4, 256, LOW), BF16),
            pltpu.VMEM((4, 256, LOW), BF16),
            pltpu.VMEM((256, LOW), F32),
            pltpu.VMEM((2, LOW, 128), F32),
            pltpu.VMEM((2, LOW), F32),
        ]
        + [dma((PEERS,))] * 6
        + [dma((5,))]
        + [dma((4,))] * 12
        + [dma((8,))] * 2,
        compiler_params=pltpu.CompilerParams(collective_id=1, has_side_effects=True, vmem_limit_bytes=58 << 20),
        name="embedding_step",
    )(ids, cot, table, accum)
    return (pooled.reshape(samples, tables, 128), new_table.reshape(2, 8 * LOW, 128), new_accum)


def solution(mesh):
    in_specs = (
        P("mod", "rep", None),
        P("mod", "rep"),
        P(("rep", "mod"), None, None),
        P(("rep", "mod"), None, None),
    )
    out_specs = (P(("rep", "mod"), None, None), P("mod", None, None), P("mod", None))
    return jax.shard_map(local, mesh=mesh, in_specs=in_specs, out_specs=out_specs, check_vma=False)
```

time: 515 us -> 131 us (0.25)
  matrix products: 291 us -> 0 us
  Pallas kernels: 0 us -> 121 us
  waiting for transfers between devices: 95.8 us -> 0 us
  blocking collectives: 38.3 us -> 0 us
  starting transfers between devices: 21.3 us -> 0 us
  local copies, waits for them, and re-layouts: 25.8 us -> 5.16 us
  other arithmetic: 16.1 us -> 1.78 us
  between operations: 14.4 us -> 0.65 us
  loops' own time: 7.22 us -> 0 us
    dot_general x32 -> x0, matrix products: 291 us -> none  [the longest x16 149 us: step(): jnp.dot(counts_low, lookup[owned_index], preferred_element_type=jnp.float32)]
    pallas_call x0 -> x1, Pallas kernels: none -> 121 us  [local(): pl.pallas_call(step_kernel, out_shape=[jax.ShapeDtypeStruct((samples, pai...]
    all_gather x1 -> x0, waiting for transfers between devices: 46.6 us -> none  [local(): lax.all_gather(table, 'rep', axis=1, tiled=True)]
    psum x1 -> x0, waiting for transfers between devices: 41.7 us -> none  [local(): total = lax.psum(row_grad.astype(jnp.bfloat16), 'rep').astype(jnp.float32)]
    all_gather x1 -> x0, blocking collectives: 38.3 us -> none  [local(): lax.all_gather(accum, 'rep', axis=1, tiled=True)]
    all_to_all x3 -> x0, starting transfers between devices: 21.2 us -> none  [the longest x1 9.23 us: local(): lax.all_to_all(bag_rows, 'mod', split_axis=1, concat_axis=0, tiled=True)]
    squeeze x16 -> x0, local copies, waits for them, and re-layouts: 7.8 us -> none  [the longest x8 7.74 us: pool_and_grad(): row_grad, pooled_blocks = lax.scan(step, start, (ids_blocks, cot_blocks))]
    another operation x1 -> x0, loops' own time: 7.22 us -> none  [pool_and_grad(): row_grad, pooled_blocks = lax.scan(step, start, (ids_blocks, cot_blocks))]
  transfers between devices with their start and end apart: 5 -> 0, of which waited for: 3 -> 0; matrix products, arithmetic and copies ran while one was open for 3% -> 0% of each run, Pallas kernels for 0% -> 0%
where the time goes in v2:
time: 131 us; the launch traced here: 128 us
  Pallas kernels  121 us (92%)
  local copies, waits for them, and re-layouts  5.16 us (4%)
  other arithmetic  1.78 us (1%)
    pallas_call x1, Pallas kernels, local(): pl.pallas_call(step_kernel, out_shape=[jax.ShapeDtypeStruct((samples, pai...  121 us
    unnamed x7, local copies, waits for them, and re-layouts  5.16 us

profile of v2, /device:TPU:1, one launch (start us, length us, event | category | flops | bytes accessed | tf_op | source)
XLA Modules:
  0.0 128.1 jit_solution(1756410198754455771)
XLA Ops:
  0.6 1.8 %convert_element_type.6 = s16[128,64,16]{0,2,1:T(8,128)(2,1)} convert(s32[128,64,16]{0,2,1:T(8,128)} %param.6) | non-fusion elementwise | flops 131072 | bytes 786432 | tf_op jit(solution)/shard_map/convert_element_type | solution.py:317
  2.4 120.5 %embedding_step.1 = (bf16[128,32,2,128]{3,2,1,0:T(2,128)(2,1)}, f32[2,8,256,128]{3,2,1,0:T(8,128)}, f32[2,2048]{1,0:T(2,128)}) custom-call(s16[32,32,128]{2,1,0:T(8,128)(2,1)} %bitcast.9, bf16[128,32,2,128]{3,2,1,0:T(2,128)(2,1)} %bitcast.6, f32[2,256,128]{2,1,0:T(8,128)} %table_ref.1, f32[2,256]{1,0:T(2,128)} %accum_ref.1), custom_call_target="tpu_custom_call" | custom-call | tf_op jit(solution)/shard_map/embedding_step/pallas_call | solution.py:321
  122.9 0.0 copy-start
  122.9 3.2 %copy.10 = bf16[128,64,128]{2,1,0:T(8,128)(2,1)} copy(bf16[128,64,128]{2,1,0:T(8,128)(2,1)} %bitcast.8) | data formatting | bytes 4194304
  126.2 0.0 copy-done
  126.2 0.0 copy-start.1
  126.2 1.3 %copy.11 = f32[2,2048,128]{2,1,0:T(8,128)} copy(f32[2,2048,128]{2,1,0:T(8,128)S(1)} %bitcast.7) | data formatting | bytes 4194304
  127.5 0.0 copy-done.1
  127.5 0.6 copy.12
Async XLA Ops:
  122.9 3.2 %copy-start = (f32[2,8,256,128]{3,2,1,0:T(8,128)S(1)}, f32[2,8,256,128]{3,2,1,0:T(8,128)}, u32[]{:S(2)}) copy-start(f32[2,8,256,128]{3,2,1,0:T(8,128)} %get-tuple-element.7) | copy-start | bytes 6291460
  126.2 1.3 %copy-start.1 = (f32[2,2048]{1,0:T(2,128)S(1)}, f32[2,2048]{1,0:T(2,128)}, u32[]{:S(2)}) copy-start(f32[2,2048]{1,0:T(2,128)} %get-tuple-element.14) | copy-start | bytes 49156

commit v3 on v2

v3 whole, which is shorter than its diff:
```python
import functools

import jax
import jax.numpy as jnp
from jax import lax
from jax.experimental import pallas as pl
from jax.experimental.pallas import tpu as pltpu
from jax.sharding import PartitionSpec as P

BF16, F32, I32 = jnp.bfloat16, jnp.float32, jnp.int32
SUB = 8
HIGH = 16
LOW = 128
SHARD = 256
PEERS = 32
CHUNK = 256
BATCHED = 4
GROUPS = PEERS // BATCHED
EARLY, MIDDLE, LATE = 4, 6, 8
STRIDE = 11
MESH = pl.DeviceIdType.MESH


def away(me, step, sign):
    x, y, z = me // 8, (me // 2) % 4, me % 2
    dx, dy, dz = step // 8, (step // 2) % 4, step % 2
    return ((x + sign * dx + 4) % 4) * 8 + ((y + sign * dy + 4) % 4) * 2 + (z + dz) % 2


def order(i):
    return (i * STRIDE) % PEERS


def step_kernel(
    wide_ids_ref, cot_ref, table_ref, accum_ref, pooled_ref, new_table_ref, new_accum_ref,
    ids_ref, ids_buf, cot_buf, pooled_buf, shards, both, high_key, low_key, counts, split,
    pair_out, pair_in, far_out, far_in, near_out, near_in, new_shard, new_sums,
    ids_out, ids_in, cot_out, cot_in, pool_out, pool_in, local_sem,
    tab_out, tab_in, tab_twin_out, tab_twin_in, px_out, px_in, far_sem_out, far_sem_in, near_sem_out, near_sem_in,
    new_out, new_in, new_twin_out, new_twin_in, acc_out, acc_in,
):
    me = lax.axis_index("mod")
    rep = lax.axis_index("rep")
    high, core = rep // 2, rep % 2
    twin = {"rep": high * 2 + 1 - core}

    x, y, z = me // 8, (me // 2) % 4, me % 2
    xs = [((x + d) % 4) * 8 for d in range(4)]
    ys = [((y + d) % 4) * 2 for d in range(4)]
    zs = [(z + d) % 2 for d in range(2)]

    def peer(k, sign):
        if not isinstance(k, int):
            return away(me, k, sign)
        return xs[(sign * (k // 8)) % 4] + ys[(sign * (k // 2)) % 4] + zs[k % 2]

    def ring(step):
        return {"rep": ((high + step + 4) % 4) * 2 + core}

    def remote(src, dst, out_sem, in_sem, device):
        return pltpu.make_async_remote_copy(
            src_ref=src, dst_ref=dst, send_sem=out_sem, recv_sem=in_sem, device_id=device, device_id_type=MESH
        )

    def ids_copy(k):
        return remote(ids_ref.at[peer(k, 1)], ids_buf.at[k], ids_out.at[k], ids_in.at[k], {"mod": peer(k, 1)})

    def cot_copy(k):
        return remote(cot_ref.at[:, peer(k, 1)], cot_buf.at[k], cot_out.at[k], cot_in.at[k], {"mod": peer(k, 1)})

    def pool_copy(k):
        return remote(pooled_buf.at[k], pooled_ref.at[:, me], pool_out.at[k], pool_in.at[k], {"mod": peer(k, -1)})

    def pool_arrival(k):
        return remote(
            pooled_buf.at[k], pooled_ref.at[:, peer(k, 1)], pool_out.at[k], pool_in.at[k], {"mod": peer(k, -1)}
        )

    def slot(offset, other=0):
        return ((high + offset + 4) % 4) * 2 + (core + other - 2 * core * other)

    def ring_near(ref, n, out_sem, in_sem, arrival=False):
        table, side = (n, 1) if n < 2 else (3 - n, -1)
        at = ref.at[table, slot(-side if arrival else 0)]
        return remote(at, at, out_sem.at[n], in_sem.at[n], ring(side))

    def ring_far(ref, n, out_sem, in_sem, arrival=False):
        table, side = (0, 1) if n == 0 else (1, -1)
        at = ref.at[table, slot(2 if arrival else -side)]
        return remote(at, at, out_sem.at[4 + n], in_sem.at[4 + n], ring(side))

    def twin_copy(ref, offset, table, out_sem, in_sem, arrival=False):
        at = ref.at[table, slot(offset, 1 if arrival else 0)]
        n = (offset + 4) % 4 * 2 + table
        return remote(at, at, out_sem.at[n], in_sem.at[n], twin)

    def spread_own(ref, out_sem, in_sem, twin_out, twin_in):
        for n in (0, 2, 1, 3):
            ring_near(ref, n, out_sem, in_sem).start()
        for table in range(2):
            twin_copy(ref, 0, table, twin_out, twin_in).start()

    def spread_near(ref, out_sem, in_sem, twin_out, twin_in):
        for n in range(2):
            ring_near(ref, 2 * n, out_sem, in_sem, True).wait_recv()
            ring_far(ref, n, out_sem, in_sem).start()
            twin_copy(ref, -1 if n == 0 else 1, n, twin_out, twin_in).start()

    def spread_rest(ref, out_sem, in_sem, twin_out, twin_in):
        for n in range(2):
            ring_near(ref, 2 * n + 1, out_sem, in_sem, True).wait_recv()
            twin_copy(ref, -1 if n == 0 else 1, 1 - n, twin_out, twin_in).start()
        for n in range(2):
            ring_far(ref, n, out_sem, in_sem, True).wait_recv()
            twin_copy(ref, 2, n, twin_out, twin_in).start()

    def spread_end(ref, twin_out, twin_in):
        for offset in range(4):
            for table in range(2):
                twin_copy(ref, offset, table, twin_out, twin_in, True).wait_recv()

    def spread_sent(ref, out_sem, in_sem, twin_out, twin_in):
        for n in range(4):
            ring_near(ref, n, out_sem, in_sem).wait_send()
        for n in range(2):
            ring_far(ref, n, out_sem, in_sem).wait_send()
        for offset in range(4):
            for table in range(2):
                twin_copy(ref, offset, table, twin_out, twin_in).wait_send()

    barrier = pltpu.get_barrier_semaphore()

    for k in range(1, PEERS):
        pl.semaphore_signal(barrier, inc=1, device_id={"mod": peer(k, 1)}, device_id_type=MESH)
    for r in range(1, 8):
        pl.semaphore_signal(barrier, inc=1, device_id={"rep": (rep + r) % 8}, device_id_type=MESH)

    own_cot = pltpu.make_async_copy(cot_ref.at[:, me], cot_buf.at[0], local_sem.at[1])
    own_cot.start()

    @pl.loop(0, PEERS)
    def _(k):
        ids_ref[k] = wide_ids_ref[k].astype(jnp.int16)

    ids_buf[0] = ids_ref[me]
    shards[0, rep] = table_ref[0].astype(BF16)
    shards[1, rep] = table_ref[1].astype(BF16)
    pl.semaphore_wait(barrier, PEERS - 1 + 7)

    for i in range(1, PEERS):
        ids_copy(order(i)).start()

    spread_own(shards, tab_out, tab_in, tab_twin_out, tab_twin_in)

    for i in range(1, PEERS):
        cot_copy(order(i)).start()

    own_cot.wait()

    lane = lax.broadcasted_iota(I32, (16, 256), 1)
    iota = lax.broadcasted_iota(I32, (16, 256), 0).astype(F32)
    one, zero = jnp.ones((16, 256), BF16), jnp.zeros((16, 256), BF16)
    sample3 = lax.broadcasted_iota(I32, (16, SUB, 128), 1)
    lane3 = lax.broadcasted_iota(I32, (16, SUB, 128), 2) // 32

    def count_chunks(first):
        for c in range(2):
            i = first + c
            k = order(i)

            if c > 0:
                ids_copy(k).wait_recv()
            else:

                @pl.when(i > 0)
                def _(k=k):
                    ids_copy(k).wait_recv()

        for c in range(2):
            ids = ids_buf[order(first + c)].astype(I32).astype(F32)
            turned = jnp.concatenate([ids] * 4, 0).T.reshape(16, SUB, 128)
            upper = jnp.sum(jnp.where(sample3 == lane3, turned, 0.0), axis=1)
            lower = jnp.sum(jnp.where(sample3 == lane3 + 4, turned, 0.0), axis=1)
            flat = jnp.concatenate([upper, lower], 1).astype(I32)
            high_key[c * 16 : (c + 1) * 16] = ((flat // LOW) * 16 + lane // 16).astype(F32)
            low_key[c * 16 : (c + 1) * 16] = (flat % LOW).astype(F32)
        base = pl.multiple_of(first * CHUNK, 2 * CHUNK)
        for b in range(32):
            high_row = jnp.broadcast_to(high_key[b : b + 1, :], (16, 256)).astype(BF16)
            low_row = jnp.broadcast_to(low_key[b : b + 1, :], (16, 256)).astype(BF16)
            high_hot = jnp.concatenate(
                [jnp.where(high_row == (iota + 16 * j).astype(BF16), one, zero) for j in range(HIGH)], 0
            )
            low_hot = jnp.concatenate(
                [jnp.where(low_row == (iota + 16 * j).astype(BF16), one, zero) for j in range(LOW // 16)], 0
            )
            out = lax.dot_general(high_hot, low_hot, (((1,), (1,)), ((), ())), preferred_element_type=F32).astype(BF16)
            for j in range(HIGH):
                counts[j, pl.ds(base + b * 16, 16), :] = out[j * 16 : (j + 1) * 16]

    parity = lax.broadcasted_iota(I32, (BATCHED * CHUNK, 128), 0) % 2
    odd = (lax.broadcasted_iota(I32, (128, CHUNK), 1) % 2).astype(F32).astype(BF16)

    def pool_group(g):
        base = pl.multiple_of(g * BATCHED * CHUNK, BATCHED * CHUNK)
        rows = jnp.concatenate([counts[j, pl.ds(base, BATCHED * CHUNK), :] for j in range(HIGH)], 1)
        sums = jnp.dot(rows, both[...], preferred_element_type=F32)
        picked = jnp.where(parity == 0, sums[:, :128], sums[:, 128:]).astype(BF16)
        for b in range(BATCHED):
            pooled_buf[order(g * BATCHED + b)] = picked[b * CHUNK : (b + 1) * CHUNK].reshape(CHUNK // 2, 2, 128)
        for b in range(BATCHED):
            i = g * BATCHED + b

            @pl.when(i > 0)
            def _(i=i):
                pool_copy(order(i)).start()

    def pool_groups(start, end):
        if end > start:

            @pl.loop(start, end)
            def _(g):
                pool_group(g)

    def turn_cotangents(g):
        @pl.loop(0, BATCHED)
        def _(b):
            i = g * BATCHED + b
            k = order(i)

            @pl.when(i > 0)
            def _():
                cot_copy(k).wait_recv()

            turned = cot_buf[k].reshape(CHUNK, 128).T
            at = pl.ds(pl.multiple_of(i * CHUNK, CHUNK), CHUNK)
            second = turned * odd
            split[0:128, at] = turned - second
            split[128:256, at] = second

    @pl.loop(0, GROUPS)
    def _(g):
        @pl.loop(0, BATCHED // 2)
        def _(b):
            count_chunks(g * BATCHED + 2 * b)

        @pl.when(g == 3)
        def _():
            spread_near(shards, tab_out, tab_in, tab_twin_out, tab_twin_in)

        @pl.when(g == 6)
        def _():
            spread_rest(shards, tab_out, tab_in, tab_twin_out, tab_twin_in)

    spread_end(shards, tab_twin_out, tab_twin_in)
    for j in range(8):
        both[j * SHARD : (j + 1) * SHARD, :] = jnp.concatenate([shards[0, j], shards[1, j]], 1)

    @pl.loop(0, EARLY)
    def _(g):
        pool_group(g)

    own_pool = pltpu.make_async_copy(pooled_buf.at[0], pooled_ref.at[:, me], local_sem.at[2])
    own_pool.start()

    @pl.loop(0, GROUPS)
    def _(g):
        turn_cotangents(g)

    def grad_block(at):
        pieces = [counts[at * (SHARD // LOW) + j] for j in range(SHARD // LOW)]
        return jnp.dot(split[...], jnp.concatenate(pieces, 1), preferred_element_type=F32)

    def pair_copy(step):
        return remote(pair_out.at[step], pair_in.at[step], px_out.at[step], px_in.at[step], twin)

    def far_copy(n):
        return remote(far_out.at[n], far_in.at[n], far_sem_out.at[n], far_sem_in.at[n], ring(1 - 2 * n))

    def near_copy(n):
        return remote(near_out.at[n], near_in.at[n], near_sem_out.at[n], near_sem_in.at[n], ring(1 - 2 * n))

    def twin_block(step):
        pair_out[step] = grad_block(slot(step, 1)).astype(BF16)
        pair_copy(step).start()

    def own_block(step):
        own = grad_block(slot(step))
        pair_copy(step).wait_recv()
        return own + pair_in[step].astype(F32)

    twin_block(2)
    twin_block(1)
    total = own_block(2)
    for n in range(2):
        far_out[n] = total[n * 128 : (n + 1) * 128].astype(BF16)
        far_copy(n).start()
    twin_block(3)
    twin_block(0)
    pool_groups(EARLY, MIDDLE)
    for n in range(2):
        total = own_block(1 + 2 * n)
        far_copy(n).wait_recv()
        mine = slice(n * 128, (n + 1) * 128)
        rest = slice((1 - n) * 128, (2 - n) * 128)
        near_out[n, mine] = (total[mine] + far_in[n].astype(F32)).astype(BF16)
        near_out[n, rest] = total[rest].astype(BF16)
        near_copy(n).start()
    grad = own_block(0)
    pool_groups(MIDDLE, LATE)
    for n in range(2):
        near_copy(n).wait_recv()
        grad = grad + near_in[n].astype(F32)
    for t in range(2):
        one_grad = grad[t * 128 : (t + 1) * 128]
        sums = accum_ref[t : t + 1, :] + jnp.mean(one_grad * one_grad, axis=0, keepdims=True)
        new_sums[t : t + 1, :] = sums
        new_shard[t, rep] = table_ref[t] - (0.1 * one_grad / jnp.sqrt(sums)).T

    here = pl.ds(pl.multiple_of(rep * SHARD, SHARD), SHARD)
    own_sums = pltpu.make_async_copy(new_sums, new_accum_ref.at[:, here], local_sem.at[4])

    def sums_copy(r, at):
        where = pl.ds(pl.multiple_of(at * SHARD, SHARD), SHARD)
        return remote(new_sums, new_accum_ref.at[:, where], acc_out.at[r], acc_in.at[r], {"rep": (rep + r) % 8})

    spread = (new_out, new_in, new_twin_out, new_twin_in)
    spread_own(new_shard, *spread)

    for r in range(1, 8):
        sums_copy(r, rep).start()

    own_sums.start()
    pool_groups(LATE, GROUPS)
    spread_near(new_shard, *spread)
    spread_rest(new_shard, *spread)
    spread_end(new_shard, new_twin_out, new_twin_in)
    own_new = pltpu.make_async_copy(new_shard, new_table_ref, local_sem.at[3])
    own_new.start()

    @pl.loop(1, 8)
    def _(r):
        sums_copy(r, (rep - r + 8) % 8).wait_recv()

    for i in range(1, PEERS):
        pool_arrival(order(i)).wait_recv()

    own_pool.wait()
    own_new.wait()
    own_sums.wait()

    for k in range(1, PEERS):
        ids_copy(k).wait_send()
        cot_copy(k).wait_send()
        pool_copy(k).wait_send()

    spread_sent(shards, tab_out, tab_in, tab_twin_out, tab_twin_in)
    spread_sent(new_shard, *spread)
    for n in range(2):
        far_copy(n).wait_send()
        near_copy(n).wait_send()
    for step in range(4):
        pair_copy(step).wait_send()

    @pl.loop(1, 8)
    def _(r):
        sums_copy(r, rep).wait_send()


def local(table, accum, bag_rows, pooled_grad):
    samples, tables, pool_len = bag_rows.shape
    pairs = tables // 2
    ids = bag_rows.transpose(1, 2, 0).reshape(pairs, 2 * pool_len, samples)
    cot = pooled_grad.reshape(samples, pairs, 2, 128)
    rows = PEERS * CHUNK
    dma = pltpu.SemaphoreType.DMA
    pooled, new_table, new_accum = pl.pallas_call(
        step_kernel,
        out_shape=[
            jax.ShapeDtypeStruct((samples, pairs, 2, 128), BF16),
            jax.ShapeDtypeStruct((2, 8, SHARD, 128), F32),
            jax.ShapeDtypeStruct((2, 8 * SHARD), F32),
        ],
        in_specs=[
            pl.BlockSpec(memory_space=pltpu.VMEM),
            pl.BlockSpec(memory_space=pl.ANY),
            pl.BlockSpec(memory_space=pltpu.VMEM),
            pl.BlockSpec(memory_space=pltpu.VMEM),
        ],
        out_specs=[pl.BlockSpec(memory_space=pl.ANY)] * 3,
        scratch_shapes=[
            pltpu.VMEM((PEERS, 32, 128), jnp.int16),
            pltpu.VMEM((PEERS, 32, 128), jnp.int16),
            pltpu.VMEM((PEERS, CHUNK // 2, 2, 128), BF16),
            pltpu.VMEM((PEERS, CHUNK // 2, 2, 128), BF16),
            pltpu.VMEM((2, 8, SHARD, 128), BF16),
            pltpu.VMEM((HIGH * LOW, 256), BF16),
            pltpu.VMEM((32, 256), F32),
            pltpu.VMEM((32, 256), F32),
            pltpu.VMEM((HIGH, rows, LOW), BF16),
            pltpu.VMEM((256, rows), BF16),
            pltpu.VMEM((4, 256, SHARD), BF16),
            pltpu.VMEM((4, 256, SHARD), BF16),
            pltpu.VMEM((2, 128, SHARD), BF16),
            pltpu.VMEM((2, 128, SHARD), BF16),
            pltpu.VMEM((2, 256, SHARD), BF16),
            pltpu.VMEM((2, 256, SHARD), BF16),
            pltpu.VMEM((2, 8, SHARD, 128), F32),
            pltpu.VMEM((2, SHARD), F32),
        ]
        + [dma((PEERS,))] * 6
        + [dma((5,))]
        + [dma((8,))] * 4
        + [dma((4,))] * 6
        + [dma((8,))] * 6,
        compiler_params=pltpu.CompilerParams(collective_id=1, has_side_effects=True, vmem_limit_bytes=58 << 20),
        name="embedding_step",
    )(ids, cot, table, accum)
    return (pooled.reshape(samples, tables, 128), new_table.reshape(2, 8 * SHARD, 128), new_accum)


def solution(mesh):
    in_specs = (
        P("mod", "rep", None),
        P("mod", "rep"),
        P(("rep", "mod"), None, None),
        P(("rep", "mod"), None, None),
    )
    out_specs = (P(("rep", "mod"), None, None), P("mod", None, None), P("mod", None))
    return jax.shard_map(local, mesh=mesh, in_specs=in_specs, out_specs=out_specs, check_vma=False)
```

time: 131 us -> 121 us (0.924); the launches traced: 128 us -> 121 us
  Pallas kernels: 121 us -> 116 us
  other arithmetic: 1.78 us -> 0 us
    pallas_call x1, Pallas kernels: 121 us -> 116 us  [local(): pl.pallas_call(step_kernel, out_shape=[jax.ShapeDtypeStruct((samples, pai...]
    convert_element_type x1 -> x0, other arithmetic: 1.78 us -> none  [local(): bag_rows.transpose(1, 2, 0).astype(jnp.int16)]
where the time goes in v3:
time: 121 us
  Pallas kernels  116 us (96%)
  local copies, waits for them, and re-layouts  5.16 us (4%)
    pallas_call x1, Pallas kernels, local(): pl.pallas_call(step_kernel, out_shape=[jax.ShapeDtypeStruct((samples, pai...  116 us
    unnamed x7, local copies, waits for them, and re-layouts  5.16 us

profile of v3, /device:TPU:1, one launch (start us, length us, event | category | flops | bytes accessed | tf_op | source)
XLA Modules:
  0.0 121.3 jit_solution(10801272594616240907)
XLA Ops:
  0.6 115.5 %embedding_step.1 = (bf16[128,32,2,128]{3,2,1,0:T(2,128)(2,1)}, f32[2,8,256,128]{3,2,1,0:T(8,128)}, f32[2,2048]{1,0:T(2,128)}) custom-call(s32[32,32,128]{2,1,0:T(8,128)} %bitcast.9, bf16[128,32,2,128]{3,2,1,0:T(2,128)(2,1)} %bitcast.6, f32[2,256,128]{2,1,0:T(8,128)} %table_ref.1, f32[2,256]{1,0:T(2,128)} %accum_ref.1), custom_call_target="tpu_custom_call" | custom-call | tf_op jit(solution)/shard_map/embedding_step/pallas_call | solution.py:377
  116.1 0.0 copy-start
  116.1 3.2 %copy.10 = bf16[128,64,128]{2,1,0:T(8,128)(2,1)} copy(bf16[128,64,128]{2,1,0:T(8,128)(2,1)} %bitcast.8) | data formatting | bytes 4194304
  119.4 0.0 copy-done
  119.4 0.0 copy-start.1
  119.4 1.3 %copy.11 = f32[2,2048,128]{2,1,0:T(8,128)} copy(f32[2,2048,128]{2,1,0:T(8,128)S(1)} %bitcast.7) | data formatting | bytes 4194304
  120.7 0.0 copy-done.1
  120.7 0.6 copy.12
Async XLA Ops:
  116.1 3.2 %copy-start = (f32[2,8,256,128]{3,2,1,0:T(8,128)S(1)}, f32[2,8,256,128]{3,2,1,0:T(8,128)}, u32[]{:S(2)}) copy-start(f32[2,8,256,128]{3,2,1,0:T(8,128)} %get-tuple-element.7) | copy-start | bytes 6291460
  119.4 1.3 %copy-start.1 = (f32[2,2048]{1,0:T(2,128)S(1)}, f32[2,2048]{1,0:T(2,128)}, u32[]{:S(2)}) copy-start(f32[2,2048]{1,0:T(2,128)} %get-tuple-element.14) | copy-start | bytes 49156

commit v4 on v3

--- a/solution.py
+++ b/solution.py
@@ -16,7 +16,7 @@
 CHUNK = 256
 BATCHED = 4
 GROUPS = PEERS // BATCHED
-EARLY, MIDDLE, LATE = 4, 6, 8
+EARLY, MIDDLE, LATE = 6, 8, 8
 STRIDE = 11
 MESH = pl.DeviceIdType.MESH
 
@@ -332,8 +332,13 @@
 
     own_sums.start()
     pool_groups(LATE, GROUPS)
+    for k in range(1, PEERS):
+        ids_copy(k).wait_send()
+        cot_copy(k).wait_send()
     spread_near(new_shard, *spread)
     spread_rest(new_shard, *spread)
+    for i in range(1, PEERS):
+        pool_arrival(order(i)).wait_recv()
     spread_end(new_shard, new_twin_out, new_twin_in)
     own_new = pltpu.make_async_copy(new_shard, new_table_ref, local_sem.at[3])
     own_new.start()
@@ -342,16 +347,12 @@
     def _(r):
         sums_copy(r, (rep - r + 8) % 8).wait_recv()
 
-    for i in range(1, PEERS):
-        pool_arrival(order(i)).wait_recv()
 
     own_pool.wait()
     own_new.wait()
     own_sums.wait()
 
     for k in range(1, PEERS):
-        ids_copy(k).wait_send()
-        cot_copy(k).wait_send()
         pool_copy(k).wait_send()
 
     spread_sent(shards, tab_out, tab_in, tab_twin_out, tab_twin_in)

time: 121 us -> 120 us (level); the launches traced: 121 us -> 118 us
  Pallas kernels: 116 us -> 112 us
    pallas_call x1, Pallas kernels: 116 us -> 112 us  [local(): pl.pallas_call(step_kernel, out_shape=[jax.ShapeDtypeStruct((samples, pai...]
where the time goes in v4:
time: 120 us; the launch traced here: 118 us
  Pallas kernels  112 us (93%)
  local copies, waits for them, and re-layouts  5.16 us (4%)
    pallas_call x1, Pallas kernels, local(): pl.pallas_call(step_kernel, out_shape=[jax.ShapeDtypeStruct((samples, pai...  112 us
    unnamed x7, local copies, waits for them, and re-layouts  5.16 us

profile of v4, /device:TPU:1, one launch (start us, length us, event | category | flops | bytes accessed | tf_op | source)
XLA Modules:
  0.0 118.2 jit_solution(3363176040574063225)
XLA Ops:
  0.6 112.4 %embedding_step.1 = (bf16[128,32,2,128]{3,2,1,0:T(2,128)(2,1)}, f32[2,8,256,128]{3,2,1,0:T(8,128)}, f32[2,2048]{1,0:T(2,128)}) custom-call(s32[32,32,128]{2,1,0:T(8,128)} %bitcast.9, bf16[128,32,2,128]{3,2,1,0:T(2,128)(2,1)} %bitcast.6, f32[2,256,128]{2,1,0:T(8,128)} %table_ref.1, f32[2,256]{1,0:T(2,128)} %accum_ref.1), custom_call_target="tpu_custom_call" | custom-call | tf_op jit(solution)/shard_map/embedding_step/pallas_call | solution.py:378
  113.0 0.0 copy-start
  113.0 3.2 %copy.10 = bf16[128,64,128]{2,1,0:T(8,128)(2,1)} copy(bf16[128,64,128]{2,1,0:T(8,128)(2,1)} %bitcast.8) | data formatting | bytes 4194304
  116.3 0.0 copy-done
  116.3 0.0 copy-start.1
  116.3 1.3 %copy.11 = f32[2,2048,128]{2,1,0:T(8,128)} copy(f32[2,2048,128]{2,1,0:T(8,128)S(1)} %bitcast.7) | data formatting | bytes 4194304
  117.6 0.0 copy-done.1
  117.6 0.6 copy.12
Async XLA Ops:
  113.0 3.2 %copy-start = (f32[2,8,256,128]{3,2,1,0:T(8,128)S(1)}, f32[2,8,256,128]{3,2,1,0:T(8,128)}, u32[]{:S(2)}) copy-start(f32[2,8,256,128]{3,2,1,0:T(8,128)} %get-tuple-element.7) | copy-start | bytes 6291460
  116.3 1.3 %copy-start.1 = (f32[2,2048]{1,0:T(2,128)S(1)}, f32[2,2048]{1,0:T(2,128)}, u32[]{:S(2)}) copy-start(f32[2,2048]{1,0:T(2,128)} %get-tuple-element.14) | copy-start | bytes 49156
